TPU v7x, 32 devices: a whole 2x2x4 slice. The times are simulated.
32 devices in a mesh: groups: 2 (over y), tensor: 4 (over z), section: 2 (over x), seq: 2 (over core).
Axes of the slice: x: 2, y: 2, z: 4, core: 2. Of those that a mesh axis runs over, the one named last changes fastest.
Arguments:
- token_ids: int32 [4, 96], P('groups'), parts along dimension 0, may hold values from 0 to 511
- leading_span_index: int32 [2], P('groups'), parts along dimension 0, may hold values from 8 to 4103
- embed_table: float32 [512, 8192], P(None, 'tensor'), may hold values from -6 to 6
- norm_gain: float32 [2, 8192], P('section', 'tensor'), may hold values from 0.25 to 1.75
- decay_rates: float32 [2, 16, 8192], P('section', None, 'tensor'), may hold values from 0.0002 to 0.03
- residues: float32 [2, 16, 8192], P('section', None, 'tensor'), may hold values from -0.12 to 0.12
- history: float32 [2, 8, 192, 8192], P('section', 'seq', 'groups', 'tensor'), parts along dimension 2, may hold values from -6 to 6
- mix_weight: bfloat16 [2, 8192, 8192], P('section', None, ('tensor', 'seq')), may hold values from -0.0625 to 0.0625
Outputs:
- section_out: float32 [2, 2, 192, 8192], P('section', None, 'groups', ('tensor', 'seq')), parts along dimension 2
There are 2 independent parts, one for each index of `groups`. A program takes and returns all parts, laid end to end along the dimension named above; an argument that names none is the same for every part. Nothing has to cross between parts.
Inputs may be any that keep to these rules, and one draw needn't show every extreme that they name: `leading_span_index`: index of the first span of the run; the span before it is the newest one in history.
All inputs are finite; a program needn't handle non-finite values.
Results may differ from a plain program's by a relative error of at most 0.0036.
Values may be sent and summed in bfloat16 or wider, within the bound.
A program may use at most 128 MiB of HBM per device.

v0:
```python
import functools

import jax
import jax.numpy as jnp
from jax import lax
from jax.experimental import pallas as pl
from jax.experimental.pallas import tpu as pltpu
from jax.sharding import PartitionSpec as P

epsilon = 1e-05
LANES = 128
MESH = pl.DeviceIdType.MESH


def spread(start, count, stride):
    return pl.ds(start, count, stride=stride) if count > 1 else pl.ds(start, 1)


def kernel(
    dims,
    ids_ref,
    lead_ref,
    gain_ref,
    embed_hbm,
    rates_hbm,
    residues_hbm,
    history_hbm,
    weight_hbm,
    out_ref,
    embed,
    rates,
    residues,
    history,
    weight,
    decay,
    part_send,
    part_recv,
    part_own,
    state_keep,
    x_ref,
    normed,
    conv,
    total,
    squares,
    gathered,
    x_send,
    x_recv,
    load_sem,
    part_sem,
    sq_send,
    sq_recv,
    z_send,
    z_recv,
    f_send,
    f_recv,
    s_send,
    s_recv,
):
    spans, rows, half, width, modes, slots, vocab, tensor_n, section_n, seq_n = dims
    chunks = half // LANES
    padded = (rows + LANES - 1) // LANES * LANES
    t = lax.axis_index("tensor")
    s = lax.axis_index("section")
    q = lax.axis_index("seq")
    partner = 1 - q
    me = t * seq_n + q
    peers = tensor_n * seq_n
    model_width = half * peers
    direction = 1 - 2 * ((2 * t) // tensor_n)
    first_section = s == 0
    has_next = s + 1 < section_n

    def at_tensor(step):
        return lax.rem(t + direction * step + tensor_n, tensor_n)

    def loads(with_embed):
        found = []
        for j in range(width // LANES):
            lanes = pl.ds(j * LANES, LANES)
            found.append((rates_hbm.at[0, :, lanes], rates.at[pl.ds(j * modes, modes), :], 0))
            found.append((residues_hbm.at[0, :, lanes], residues.at[pl.ds(j * modes, modes), :], 1))
            for i in range(slots):
                found.append((history_hbm.at[0, i, :, lanes], history.at[i, pl.ds(j * rows, rows), :], 2))
        return found

    barrier = pltpu.get_barrier_semaphore()

    def greet(step, carry):
        other = lax.rem(me + step, peers)
        pl.semaphore_signal(
            barrier, inc=1, device_id={"tensor": other // seq_n, "seq": other % seq_n}, device_id_type=MESH
        )
        return carry

    @pl.when(first_section)
    def _():
        for j in range(chunks):
            lanes = pl.ds(pl.multiple_of(q * half + j * LANES, LANES), LANES)
            pltpu.make_async_copy(embed_hbm.at[:, lanes], embed.at[pl.ds(j * vocab, vocab), :], load_sem.at[3]).start()

    for source, target, which in loads(False):
        pltpu.make_async_copy(source, target, load_sem.at[which]).start()
    weight_copy = pltpu.make_async_copy(weight_hbm.at[0], weight, load_sem.at[4])
    weight_copy.start()

    lax.fori_loop(1, peers, greet, 0)

    @pl.when(has_next)
    def _():
        pl.semaphore_signal(barrier, inc=1, device_id={"section": s + 1}, device_id_type=MESH)

    @pl.when(s > 0)
    def _():
        pl.semaphore_signal(barrier, inc=1, device_id={"section": s - 1}, device_id_type=MESH)

    neighbours = jnp.where(has_next, 1, 0) + jnp.where(s > 0, 1, 0)
    pl.semaphore_wait(barrier, peers - 1 + neighbours)

    def square_copy(c, source, step, send_to):
        other = lax.rem(me + step, peers)
        slot = me if send_to else other
        return pltpu.make_async_remote_copy(
            src_ref=squares.at[c, slot],
            dst_ref=squares.at[c, slot],
            send_sem=sq_send.at[c, step],
            recv_sem=sq_recv.at[c, slot],
            device_id={"tensor": other // seq_n, "seq": other % seq_n},
            device_id_type=MESH,
        )

    def share_squares(c):
        acc = jnp.zeros((rows, LANES), jnp.float32)
        for j in range(chunks):
            piece = x_ref[c, pl.ds(j * rows, rows), :]
            acc = acc + piece * piece
        if padded > rows:
            acc = jnp.concatenate([acc, jnp.zeros((padded - rows, LANES), jnp.float32)], axis=0)
        by_row = jnp.sum(acc.T, axis=0, keepdims=True)
        squares[c, me] = jnp.broadcast_to(by_row, (8, padded))

        def send(step, carry):
            square_copy(c, me, step, True).start()
            return carry

        lax.fori_loop(1, peers, send, 0)

    def embed_rows(c):
        def one(p, carry):
            x_ref[c, spread(p, chunks, rows), :] = embed[spread(ids_ref[c, p], chunks, vocab), :]
            return carry

        lax.fori_loop(0, rows, one, 0, unroll=8)
        share_squares(c)

    def arrive_rows(c):
        pltpu.make_async_remote_copy(
            src_ref=x_send.at[c],
            dst_ref=x_recv.at[c],
            send_sem=s_send.at[c],
            recv_sem=s_recv.at[c],
            device_id={"section": s - 1},
            device_id_type=MESH,
        ).wait_recv()
        for j in range(chunks):
            block = pl.ds(j * rows, rows)
            x_ref[c, block, :] = x_recv[c, block, :].astype(jnp.float32)
        share_squares(c)

    def z_copy(c, step, send_to):
        other = at_tensor(step)
        slot = me if send_to else other * seq_n + q
        return pltpu.make_async_remote_copy(
            src_ref=gathered.at[c, slot],
            dst_ref=gathered.at[c, slot],
            send_sem=z_send.at[c, other],
            recv_sem=z_recv.at[c, t if send_to else other],
            device_id={"tensor": other},
            device_id_type=MESH,
        )

    def f_copy(c, step, send_to):
        other = at_tensor(step)
        slot = other * seq_n + (q if send_to else partner)
        return pltpu.make_async_remote_copy(
            src_ref=gathered.at[c, slot],
            dst_ref=gathered.at[c, slot],
            send_sem=f_send.at[c, other],
            recv_sem=f_recv.at[c, other],
            device_id={"seq": partner},
            device_id_type=MESH,
        )

    def start_sends(c):
        f_copy(c, 0, True).start()

        def send(step, carry):
            z_copy(c, step, True).start()
            return carry

        lax.fori_loop(1, tensor_n, send, 0)

    def make_gated(c):
        def wait(step, carry):
            square_copy(c, me, step, False).wait_recv()
            return carry

        lax.fori_loop(1, peers, wait, 0)
        summed = jnp.sum(squares[c], axis=0)
        scale = lax.rsqrt(summed * (1.0 / model_width) + epsilon)
        scale = jnp.broadcast_to(scale[0:1, :], (LANES, padded)).T[:rows]
        for j in range(chunks):
            block = pl.ds(j * rows, rows)
            gain = gain_ref[0:1, pl.ds(pl.multiple_of(q * half + j * LANES, LANES), LANES)]
            normed[c, block, :] = x_ref[c, block, :] * (scale * gain)

        decays = decay[...]
        gains = jnp.stack([residues[spread(q * chunks * modes + m, chunks, modes), :] for m in range(modes)])

        def step(p, state):
            row = normed[c, spread(p, chunks, rows), :]
            state = state * decays + gains * row[None]
            conv[c, spread(p, chunks, rows), :] = jnp.sum(state, axis=0)
            return state

        state = lax.fori_loop(0, rows, step, state_keep[0], unroll=4)
        state_keep[0] = state - state_keep[1]
        for j in range(chunks):
            block = pl.ds(j * rows, rows)
            gathered[c, me, :, pl.ds(j * LANES, LANES)] = (normed[c, block, :] * conv[c, block, :]).astype(
                jnp.bfloat16
            )

    def multiply(c, slot):
        block = weight[pl.ds(pl.multiple_of(slot * half, half), half), :]
        total[...] += jnp.dot(gathered[c, slot], block, preferred_element_type=jnp.float32)

    def project(c):
        total[...] = jnp.zeros_like(total)
        multiply(c, me)

        def take(step, carry):
            z_copy(c, step, False).wait_recv()
            f_copy(c, step, True).start()
            multiply(c, at_tensor(step) * seq_n + q)
            f_copy(c, step - 1, False).wait_recv()
            multiply(c, at_tensor(step - 1) * seq_n + partner)
            return carry

        lax.fori_loop(1, tensor_n, take, 0)

    def finish(c):
        f_copy(c, tensor_n - 1, False).wait_recv()
        multiply(c, at_tensor(tensor_n - 1) * seq_n + partner)
        for j in range(chunks):
            lanes = pl.ds(j * LANES, LANES)
            block = pl.ds(j * rows, rows)
            value = x_ref[c, block, :] + total[:, lanes]
            out_ref[0, c, :, lanes] = value
            x_send[c, block, :] = value.astype(jnp.bfloat16)

        @pl.when(has_next)
        def _():
            section_copy(c).start()

    def section_copy(c):
        return pltpu.make_async_remote_copy(
            src_ref=x_send.at[c],
            dst_ref=x_recv.at[c],
            send_sem=s_send.at[c],
            recv_sem=s_recv.at[c],
            device_id={"section": s + 1},
            device_id_type=MESH,
        )

    @pl.when(first_section)
    def _():
        pltpu.make_async_copy(embed, embed, load_sem.at[3]).wait()
        for c in range(spans):
            embed_rows(c)

    pltpu.make_async_copy(rates, rates, load_sem.at[0]).wait()
    pltpu.make_async_copy(residues, residues, load_sem.at[1]).wait()
    pltpu.make_async_copy(history, history, load_sem.at[2]).wait()
    first_span = lead_ref[0]
    slot_total = slots * seq_n

    def history_part(side, target):
        rate = jnp.stack([rates[spread(side * chunks * modes + m, chunks, modes), :] for m in range(modes)])
        decay[...] = jnp.exp(-rate)
        target[...] = jnp.zeros_like(target)

        def one_slot(i, carry):
            decays = decay[...]

            def step(l, state):
                row = history[i, spread(side * chunks * rows + l, chunks, rows), :]
                return state * decays + row[None]

            state = lax.fori_loop(0, rows, step, jnp.zeros((modes, chunks, LANES), jnp.float32), unroll=8)
            age = lax.rem(first_span - 1 - (q * slots + i), slot_total) + 1
            back = ((age - 1) * rows).astype(jnp.float32)
            oldest = jnp.where(age == slot_total, 1.0, 0.0).astype(jnp.float32)
            rate = jnp.stack([rates[spread(side * chunks * modes + m, chunks, modes), :] for m in range(modes)])
            target[0] += state * jnp.exp(-rate * back)
            target[1] += state * jnp.exp(-rate * float(slot_total * rows)) * oldest
            return carry

        lax.fori_loop(0, slots, one_slot, 0)

    history_part(partner, part_send)
    part_copy = pltpu.make_async_remote_copy(
        src_ref=part_send,
        dst_ref=part_recv,
        send_sem=part_sem.at[0],
        recv_sem=part_sem.at[1],
        device_id={"seq": partner},
        device_id_type=MESH,
    )
    part_copy.start()
    history_part(q, part_own)
    part_copy.wait()
    residue = jnp.stack([residues[spread(q * chunks * modes + m, chunks, modes), :] for m in range(modes)])
    for k in range(2):
        state_keep[k] = residue * (part_own[k] + part_recv[k])

    @pl.when(jnp.logical_not(first_section))
    def _():
        arrive_rows(0)

    make_gated(0)
    start_sends(0)

    @pl.when(first_section)
    def _():
        for c in range(1, spans):
            make_gated(c)

    weight_copy.wait()
    for c in range(spans):
        project(c)

        def drain(step, carry):
            z_copy(c, step, True).wait_send()
            return carry

        lax.fori_loop(1, tensor_n, drain, 0)
        if c + 1 < spans:
            pl.when(first_section)(lambda: start_sends(c + 1))
        finish(c)
        if c + 1 < spans:

            @pl.when(jnp.logical_not(first_section))
            def _():
                arrive_rows(c + 1)
                make_gated(c + 1)
                start_sends(c + 1)

    for c in range(spans):

        def settle_f(step, carry):
            f_copy(c, step, True).wait_send()
            return carry

        def settle_q(step, carry):
            square_copy(c, me, step, True).wait_send()
            return carry

        lax.fori_loop(0, tensor_n, settle_f, 0)
        lax.fori_loop(1, peers, settle_q, 0)

        @pl.when(has_next)
        def _():
            section_copy(c).wait_send()


def local(
    token_ids,
    leading_span_index,
    embed_table,
    norm_gain,
    decay_rates,
    residues,
    history,
    mix_weight,
):
    tensor_n = lax.axis_size("tensor")
    section_n = lax.axis_size("section")
    seq_n = lax.axis_size("seq")
    spans, rows = token_ids.shape
    vocab, width = embed_table.shape
    modes = decay_rates.shape[1]
    slots = history.shape[1]
    depth, half = mix_weight.shape[1:]
    chunks = half // LANES
    peers = tensor_n * seq_n
    padded = (rows + LANES - 1) // LANES * LANES
    dims = (spans, rows, half, width, modes, slots, vocab, tensor_n, section_n, seq_n)
    f32 = jnp.float32
    smem = pl.BlockSpec(memory_space=pltpu.SMEM)
    vmem = pl.BlockSpec(memory_space=pltpu.VMEM)
    hbm = pl.BlockSpec(memory_space=pl.ANY)
    dma = pltpu.SemaphoreType.DMA
    return pl.pallas_call(
        functools.partial(kernel, dims),
        out_shape=jax.ShapeDtypeStruct((1, spans, rows, half), f32),
        in_specs=[smem, smem, vmem, hbm, hbm, hbm, hbm, hbm],
        out_specs=vmem,
        scratch_shapes=[
            pltpu.VMEM((chunks * vocab, LANES), f32),
            pltpu.VMEM((width // LANES * modes, LANES), f32),
            pltpu.VMEM((width // LANES * modes, LANES), f32),
            pltpu.VMEM((slots, width // LANES * rows, LANES), f32),
            pltpu.VMEM((depth, half), jnp.bfloat16),
            pltpu.VMEM((modes, chunks, LANES), f32),
            pltpu.VMEM((2, modes, chunks, LANES), f32),
            pltpu.VMEM((2, modes, chunks, LANES), f32),
            pltpu.VMEM((2, modes, chunks, LANES), f32),
            pltpu.VMEM((2, modes, chunks, LANES), f32),
            pltpu.VMEM((spans, chunks * rows, LANES), f32),
            pltpu.VMEM((spans, chunks * rows, LANES), f32),
            pltpu.VMEM((spans, chunks * rows, LANES), f32),
            pltpu.VMEM((rows, half), f32),
            pltpu.VMEM((spans, peers, 8, padded), f32),
            pltpu.VMEM((spans, peers, rows, half), jnp.bfloat16),
            pltpu.VMEM((spans, chunks * rows, LANES), jnp.bfloat16),
            pltpu.VMEM((spans, chunks * rows, LANES), jnp.bfloat16),
            dma((5,)),
            dma((2,)),
            dma((spans, peers)),
            dma((spans, peers)),
            dma((spans, tensor_n)),
            dma((spans, tensor_n)),
            dma((spans, tensor_n)),
            dma((spans, tensor_n)),
            dma((spans,)),
            dma((spans,)),
        ],
        compiler_params=pltpu.CompilerParams(
            collective_id=0, has_side_effects=True, vmem_limit_bytes=48 * 1024 * 1024
        ),
    )(
        token_ids,
        leading_span_index,
        norm_gain,
        embed_table,
        decay_rates,
        residues,
        history,
        mix_weight,
    )


def solution(mesh):
    placed = (
        P("groups", None),
        P("groups"),
        P(None, "tensor"),
        P("section", "tensor"),
        P("section", None, "tensor"),
        P("section", None, "tensor"),
        P("section", "seq", "groups", "tensor"),
        P("section", None, ("tensor", "seq")),
    )
    return jax.shard_map(
        local,
        mesh=mesh,
        in_specs=placed,
        out_specs=P("section", None, "groups", ("tensor", "seq")),
        check_vma=False,
    )
```

profile of v0, /device:TPU:3, one launch (start us, length us, event | category | flops | bytes accessed | tf_op | source)
XLA Modules:
  0.0 101.8 jit_solution(12061527849878344933)
XLA Ops:
  0.7 0.0 copy-start
  0.7 1.9 %copy-done = f32[1,4,96,2048]{3,2,1,0:T(8,128)S(1)} copy-done((f32[1,4,96,2048]{3,2,1,0:T(8,128)S(1)}, f32[1,4,96,2048]{3,2,1,0:T(8,128)}, u32[]{:S(2)}) %copy-start) | copy-done | bytes 3145752
  2.5 0.0 copy-start.1
  2.5 0.9 copy-done.1
  3.4 0.0 copy-start.2
  3.4 0.9 copy-done.2
  4.4 0.0 copy-start.3
  4.4 0.7 copy-done.3
  5.0 0.0 copy-start.4
  5.1 0.7 copy-done.4
  5.7 95.2 %shard_map.82 = f32[1,2,96,1024]{3,2,1,0:T(8,128)S(1)} custom-call(s32[2,96]{1,0:T(2,128)S(1)} %copy-done.4, s32[1]{0:T(128)S(6)} %copy.10.lead_ref, f32[1,2048]{1,0:T(1,128)S(1)} %copy-done.3, f32[512,2048]{1,0:T(8,128)} %embed_hbm.1, f32[1,16,2048]{2,1,0:T(8,128)S(1)} %copy-done.1, f32[1,16,2048]{2,1,0:T(8,128)S(1)} %copy-done.2, ...), custom_call_target="tpu_custom_call" | custom-call | tf_op jit(solution)/shard_map/pallas_call | solution.py:403
  100.9 0.9 copy.11
Async XLA Ops:
  0.7 1.9 %copy-start = (f32[1,4,96,2048]{3,2,1,0:T(8,128)S(1)}, f32[1,4,96,2048]{3,2,1,0:T(8,128)}, u32[]{:S(2)}) copy-start(f32[1,4,96,2048]{3,2,1,0:T(8,128)} %history_hbm.1) | copy-start | bytes 9437188
  2.5 0.9 copy-start.1
  3.4 0.9 copy-start.2
  4.4 0.7 copy-start.3
  5.0 0.7 copy-start.4
where the time goes:
time: 102 us
  Pallas kernels  95.2 us (93%)
  local copies, waits for them, and re-layouts  5.95 us (6%)
    pallas_call x1, Pallas kernels, local(): pl.pallas_call(functools.partial(kernel, dims), out_shape=jax.ShapeDtypeS...  95.2 us
    unnamed x11, local copies, waits for them, and re-layouts  5.95 us

commit v1 on v0

--- a/solution.py
+++ b/solution.py
@@ -56,7 +56,9 @@
     s_send,
     s_recv,
 ):
-    spans, rows, half, width, modes, slots, vocab, tensor_n, section_n, seq_n = dims
+    spans, parts, span_rows, half, width, modes, slots, vocab, tensor_n, section_n, seq_n = dims
+    steps = spans * parts
+    rows = span_rows // parts
     chunks = half // LANES
     padded = (rows + LANES - 1) // LANES * LANES
     t = lax.axis_index("tensor")
@@ -73,14 +75,14 @@
     def at_tensor(step):
         return lax.rem(t + direction * step + tensor_n, tensor_n)
 
-    def loads(with_embed):
+    def loads():
         found = []
         for j in range(width // LANES):
             lanes = pl.ds(j * LANES, LANES)
             found.append((rates_hbm.at[0, :, lanes], rates.at[pl.ds(j * modes, modes), :], 0))
             found.append((residues_hbm.at[0, :, lanes], residues.at[pl.ds(j * modes, modes), :], 1))
             for i in range(slots):
-                found.append((history_hbm.at[0, i, :, lanes], history.at[i, pl.ds(j * rows, rows), :], 2))
+                found.append((history_hbm.at[0, i, :, lanes], history.at[i, pl.ds(j * span_rows, span_rows), :], 2))
         return found
 
     barrier = pltpu.get_barrier_semaphore()
@@ -98,7 +100,7 @@
             lanes = pl.ds(pl.multiple_of(q * half + j * LANES, LANES), LANES)
             pltpu.make_async_copy(embed_hbm.at[:, lanes], embed.at[pl.ds(j * vocab, vocab), :], load_sem.at[3]).start()
 
-    for source, target, which in loads(False):
+    for source, target, which in loads():
         pltpu.make_async_copy(source, target, load_sem.at[which]).start()
     weight_copy = pltpu.make_async_copy(weight_hbm.at[0], weight, load_sem.at[4])
     weight_copy.start()
@@ -146,7 +148,9 @@
 
     def embed_rows(c):
         def one(p, carry):
-            x_ref[c, spread(p, chunks, rows), :] = embed[spread(ids_ref[c, p], chunks, vocab), :]
+            x_ref[c, spread(p, chunks, rows), :] = embed[
+                spread(ids_ref[c // parts, c % parts * rows + p], chunks, vocab), :
+            ]
             return carry
 
         lax.fori_loop(0, rows, one, 0, unroll=8)
@@ -223,7 +227,7 @@
             return state
 
         state = lax.fori_loop(0, rows, step, state_keep[0], unroll=4)
-        state_keep[0] = state - state_keep[1]
+        state_keep[0] = state - state_keep[1] if c % parts == parts - 1 else state
         for j in range(chunks):
             block = pl.ds(j * rows, rows)
             gathered[c, me, :, pl.ds(j * LANES, LANES)] = (normed[c, block, :] * conv[c, block, :]).astype(
@@ -235,8 +239,8 @@
         total[...] += jnp.dot(gathered[c, slot], block, preferred_element_type=jnp.float32)
 
     def project(c):
-        total[...] = jnp.zeros_like(total)
-        multiply(c, me)
+        own = weight[pl.ds(pl.multiple_of(me * half, half), half), :]
+        total[...] = jnp.dot(gathered[c, me], own, preferred_element_type=jnp.float32)
 
         def take(step, carry):
             z_copy(c, step, False).wait_recv()
@@ -255,7 +259,7 @@
             lanes = pl.ds(j * LANES, LANES)
             block = pl.ds(j * rows, rows)
             value = x_ref[c, block, :] + total[:, lanes]
-            out_ref[0, c, :, lanes] = value
+            out_ref[0, c // parts, pl.ds(c % parts * rows, rows), lanes] = value
             x_send[c, block, :] = value.astype(jnp.bfloat16)
 
         @pl.when(has_next)
@@ -275,7 +279,7 @@
     @pl.when(first_section)
     def _():
         pltpu.make_async_copy(embed, embed, load_sem.at[3]).wait()
-        for c in range(spans):
+        for c in range(steps):
             embed_rows(c)
 
     pltpu.make_async_copy(rates, rates, load_sem.at[0]).wait()
@@ -293,16 +297,16 @@
             decays = decay[...]
 
             def step(l, state):
-                row = history[i, spread(side * chunks * rows + l, chunks, rows), :]
+                row = history[i, spread(side * chunks * span_rows + l, chunks, span_rows), :]
                 return state * decays + row[None]
 
-            state = lax.fori_loop(0, rows, step, jnp.zeros((modes, chunks, LANES), jnp.float32), unroll=8)
+            state = lax.fori_loop(0, span_rows, step, jnp.zeros((modes, chunks, LANES), jnp.float32), unroll=8)
             age = lax.rem(first_span - 1 - (q * slots + i), slot_total) + 1
-            back = ((age - 1) * rows).astype(jnp.float32)
+            back = ((age - 1) * span_rows).astype(jnp.float32)
             oldest = jnp.where(age == slot_total, 1.0, 0.0).astype(jnp.float32)
             rate = jnp.stack([rates[spread(side * chunks * modes + m, chunks, modes), :] for m in range(modes)])
             target[0] += state * jnp.exp(-rate * back)
-            target[1] += state * jnp.exp(-rate * float(slot_total * rows)) * oldest
+            target[1] += state * jnp.exp(-rate * float(slot_total * span_rows)) * oldest
             return carry
 
         lax.fori_loop(0, slots, one_slot, 0)
@@ -330,24 +334,18 @@
     make_gated(0)
     start_sends(0)
 
-    @pl.when(first_section)
-    def _():
-        for c in range(1, spans):
-            make_gated(c)
-
     weight_copy.wait()
-    for c in range(spans):
+    for c in range(steps):
+        if c + 1 < steps:
+
+            @pl.when(first_section)
+            def _():
+                make_gated(c + 1)
+                start_sends(c + 1)
+
         project(c)
-
-        def drain(step, carry):
-            z_copy(c, step, True).wait_send()
-            return carry
-
-        lax.fori_loop(1, tensor_n, drain, 0)
-        if c + 1 < spans:
-            pl.when(first_section)(lambda: start_sends(c + 1))
         finish(c)
-        if c + 1 < spans:
+        if c + 1 < steps:
 
             @pl.when(jnp.logical_not(first_section))
             def _():
@@ -355,7 +353,13 @@
                 make_gated(c + 1)
                 start_sends(c + 1)
 
-    for c in range(spans):
+    for c in range(steps):
+
+        def settle_z(step, carry):
+            z_copy(c, step, True).wait_send()
+            return carry
+
+        lax.fori_loop(1, tensor_n, settle_z, 0)
 
         def settle_f(step, carry):
             f_copy(c, step, True).wait_send()
@@ -393,8 +397,11 @@
     depth, half = mix_weight.shape[1:]
     chunks = half // LANES
     peers = tensor_n * seq_n
-    padded = (rows + LANES - 1) // LANES * LANES
-    dims = (spans, rows, half, width, modes, slots, vocab, tensor_n, section_n, seq_n)
+    parts = 2 if rows % 32 == 0 else 1
+    steps = spans * parts
+    part_rows = rows // parts
+    padded = (part_rows + LANES - 1) // LANES * LANES
+    dims = (spans, parts, rows, half, width, modes, slots, vocab, tensor_n, section_n, seq_n)
     f32 = jnp.float32
     smem = pl.BlockSpec(memory_space=pltpu.SMEM)
     vmem = pl.BlockSpec(memory_space=pltpu.VMEM)
@@ -416,27 +423,27 @@
             pltpu.VMEM((2, modes, chunks, LANES), f32),
             pltpu.VMEM((2, modes, chunks, LANES), f32),
             pltpu.VMEM((2, modes, chunks, LANES), f32),
-            pltpu.VMEM((spans, chunks * rows, LANES), f32),
-            pltpu.VMEM((spans, chunks * rows, LANES), f32),
-            pltpu.VMEM((spans, chunks * rows, LANES), f32),
-            pltpu.VMEM((rows, half), f32),
-            pltpu.VMEM((spans, peers, 8, padded), f32),
-            pltpu.VMEM((spans, peers, rows, half), jnp.bfloat16),
-            pltpu.VMEM((spans, chunks * rows, LANES), jnp.bfloat16),
-            pltpu.VMEM((spans, chunks * rows, LANES), jnp.bfloat16),
+            pltpu.VMEM((steps, chunks * part_rows, LANES), f32),
+            pltpu.VMEM((steps, chunks * part_rows, LANES), f32),
+            pltpu.VMEM((steps, chunks * part_rows, LANES), f32),
+            pltpu.VMEM((part_rows, half), f32),
+            pltpu.VMEM((steps, peers, 8, padded), f32),
+            pltpu.VMEM((steps, peers, part_rows, half), jnp.bfloat16),
+            pltpu.VMEM((steps, chunks * part_rows, LANES), jnp.bfloat16),
+            pltpu.VMEM((steps, chunks * part_rows, LANES), jnp.bfloat16),
             dma((5,)),
             dma((2,)),
-            dma((spans, peers)),
-            dma((spans, peers)),
-            dma((spans, tensor_n)),
-            dma((spans, tensor_n)),
-            dma((spans, tensor_n)),
-            dma((spans, tensor_n)),
-            dma((spans,)),
-            dma((spans,)),
+            dma((steps, peers)),
+            dma((steps, peers)),
+            dma((steps, tensor_n)),
+            dma((steps, tensor_n)),
+            dma((steps, tensor_n)),
+            dma((steps, tensor_n)),
+            dma((steps,)),
+            dma((steps,)),
         ],
         compiler_params=pltpu.CompilerParams(
-            collective_id=0, has_side_effects=True, vmem_limit_bytes=48 * 1024 * 1024
+            collective_id=0, has_side_effects=True, vmem_limit_bytes=60 * 1024 * 1024
         ),
     )(
         token_ids,

time: 102 us -> 109 us (1.069)
  Pallas kernels: 95.2 us -> 106 us
  local copies, waits for them, and re-layouts: 5.95 us -> 2.09 us
    pallas_call x1, Pallas kernels: 95.2 us -> 106 us  [local(): pl.pallas_call(functools.partial(kernel, dims), out_shape=jax.ShapeDtypeS...]
    unnamed x11 -> x1, local copies, waits for them, and re-layouts: 5.95 us -> 2.09 us
where the time goes in v1:
time: 109 us; the launch traced here: 108 us
  Pallas kernels  106 us (97%)
  local copies, waits for them, and re-layouts  2.09 us (2%)
    pallas_call x1, Pallas kernels, local(): pl.pallas_call(functools.partial(kernel, dims), out_shape=jax.ShapeDtypeS...  106 us

profile of v1, /device:TPU:3, one launch (start us, length us, event | category | flops | bytes accessed | tf_op | source)
XLA Modules:
  0.0 108.3 jit_solution(14719056462726850965)
XLA Ops:
  0.7 105.6 %shard_map.82 = f32[1,2,96,1024]{3,2,1,0:T(8,128)} custom-call(s32[2,96]{1,0:T(2,128)} %ids_ref.1, s32[1]{0:T(128)S(6)} %copy.10.lead_ref, f32[1,2048]{1,0:T(1,128)} %gain_ref.1, f32[512,2048]{1,0:T(8,128)} %embed_hbm.1, f32[1,16,2048]{2,1,0:T(8,128)} %rates_hbm.1, f32[1,16,2048]{2,1,0:T(8,128)} %residues_hbm.1, f32[1,4,96,2048]{3,2,1,0:T(8,128)} %history_hbm.1, ...), custom_call_target="tpu_custom_call" | custom-call | tf_op jit(solution)/shard_map/pallas_call | solution.py:410
  106.2 2.1 %copy.11 = f32[1,2,96,1024]{3,2,1,0:T(8,128)} copy(f32[1,2,96,1024]{3,2,1,0:T(8,128)} %shard_map.82) | data formatting | bytes 1572864

commit v2 on v1

--- a/solution.py
+++ b/solution.py
@@ -338,20 +338,15 @@
     for c in range(steps):
         if c + 1 < steps:
 
-            @pl.when(first_section)
-            def _():
-                make_gated(c + 1)
-                start_sends(c + 1)
-
-        project(c)
-        finish(c)
-        if c + 1 < steps:
-
             @pl.when(jnp.logical_not(first_section))
             def _():
                 arrive_rows(c + 1)
-                make_gated(c + 1)
-                start_sends(c + 1)
+
+            make_gated(c + 1)
+            start_sends(c + 1)
+
+        project(c)
+        finish(c)
 
     for c in range(steps):
 

time: 109 us -> 92 us (0.84)
  Pallas kernels: 106 us -> 89 us
    pallas_call x1, Pallas kernels: 106 us -> 89 us  [local(): pl.pallas_call(functools.partial(kernel, dims), out_shape=jax.ShapeDtypeS...]
where the time goes in v2:
time: 92 us; the launch traced here: 91.8 us
  Pallas kernels  89 us (97%)
  local copies, waits for them, and re-layouts  2.09 us (2%)
    pallas_call x1, Pallas kernels, local(): pl.pallas_call(functools.partial(kernel, dims), out_shape=jax.ShapeDtypeS...  89 us
    unnamed x1, local copies, waits for them, and re-layouts  2.09 us

profile of v2, /device:TPU:3, one launch (start us, length us, event | category | flops | bytes accessed | tf_op | source)
XLA Modules:
  0.0 91.8 jit_solution(13007727442275413054)
XLA Ops:
  0.7 89.0 %shard_map.82 = f32[1,2,96,1024]{3,2,1,0:T(8,128)} custom-call(s32[2,96]{1,0:T(2,128)} %ids_ref.1, s32[1]{0:T(128)S(6)} %copy.10.lead_ref, f32[1,2048]{1,0:T(1,128)} %gain_ref.1, f32[512,2048]{1,0:T(8,128)} %embed_hbm.1, f32[1,16,2048]{2,1,0:T(8,128)} %rates_hbm.1, f32[1,16,2048]{2,1,0:T(8,128)} %residues_hbm.1, f32[1,4,96,2048]{3,2,1,0:T(8,128)} %history_hbm.1, ...), custom_call_target="tpu_custom_call" | custom-call | tf_op jit(solution)/shard_map/pallas_call | solution.py:405
  89.7 2.1 %copy.11 = f32[1,2,96,1024]{3,2,1,0:T(8,128)} copy(f32[1,2,96,1024]{3,2,1,0:T(8,128)} %shard_map.82) | data formatting | bytes 1572864
